TPU v7x, 256 devices: a whole 4x4x8 slice. The times are simulated.
256 devices in a mesh: seq: 32 (over z, x), head: 8 (over y, core).
Axes of the slice: x: 4, y: 4, z: 8, core: 2. Of those that a mesh axis runs over, the one named last changes fastest.
Arguments:
- mixer_input: bfloat16 [65536, 5120], P('seq', 'head'), may hold values from -6 to 6
- write_rows: bfloat16 [65536, 128], P(('seq', 'head')), may hold values from -1.796875 to 1.796875
- read_rows: bfloat16 [65536, 128], P(('seq', 'head')), may hold values from -1.796875 to 1.796875
- log_decay: float32 [80, 65536], P('head', 'seq'), may hold values from -2 to 0, as said below
- skip_gain: float32 [80], P('head'), may hold values from 0.25 to 1.75
- reset_offsets: int32 [32, 4], P('seq'), may hold values from 0 to 2048, as said below
- grad_out: bfloat16 [65536, 5120], P('seq', 'head'), may hold values from -6 to 6
Outputs:
- grad_input: bfloat16 [65536, 5120], P('seq', 'head')
- grad_write: float32 [65536, 128], P(('seq', 'head'))
- grad_read: float32 [65536, 128], P(('seq', 'head'))
Inputs may be any that keep to these rules, and one draw needn't show every extreme that they name: `log_decay`: every entry is negative. `reset_offsets`: row d lists, in increasing order, the offsets within block d of 2048 tokens at which an episode begins; unused slots hold 2048 and stand after the used ones; some row uses all 4 slots.
All inputs are finite; a program needn't handle non-finite values.
Results may differ from a plain program's by a relative error of at most 0.0055.
Values may be sent and summed in bfloat16 or wider, within the bound.
No kernel may reach another device: no remote copies, remote signals or barrier semaphores. Data moves between devices by JAX's collectives and lax.ppermute only.
A program may use at most 192 MiB of HBM per device.

v0:
```python
import jax
import jax.numpy as jnp
from jax import lax
from jax.sharding import PartitionSpec as P

SPAN = 256


def entering(part, axis, combine, identity, reverse):
    count = lax.axis_size(axis)
    place = lax.axis_index(axis)
    ahead = count - 1 - place if reverse else place
    gathered = jax.tree.map(lambda a: lax.all_gather(a, axis), part)
    state = jax.tree.map(lambda a, e: jnp.zeros_like(a) + jnp.asarray(e, a.dtype), part, identity)

    def one(step, state):
        source = count - 1 - step if reverse else step
        return combine(
            state, jax.tree.map(lambda a: lax.dynamic_index_in_dim(a, source, 0, False), gathered)
        )

    return lax.fori_loop(0, ahead, one, state)


def span_update(carry_state, inputs, skip_gain):
    feature_part, write_part, read_part, log_part, reset_part = inputs
    span_len = reset_part.shape[0]
    cum_log = jnp.cumsum(log_part, axis=1)
    reset_count = jnp.cumsum(reset_part)
    input_gain = jnp.sqrt(-jnp.expm1(2.0 * log_part))
    positions = jnp.arange(span_len)
    allowed = (positions[:, None] >= positions[None, :]) & (
        reset_count[:, None] == reset_count[None, :]
    )
    spread = cum_log[:, :, None] - cum_log[:, None, :]
    decay_matrix = jnp.exp(jnp.where(allowed[None], spread, -1e30))
    scores = jnp.dot(read_part, write_part.T, precision=lax.Precision.HIGHEST)
    weights = decay_matrix * scores[None] * input_gain[:, None, :]
    result = jnp.einsum("hts,shp->thp", weights, feature_part, precision=lax.Precision.HIGHEST)
    entry_decay = jnp.exp(cum_log) * (reset_count == 0)[None, :]
    carried = jnp.einsum("tn,hnp->thp", read_part, carry_state, precision=lax.Precision.HIGHEST)
    result = result + carried * entry_decay.T[:, :, None] + skip_gain[None, :, None] * feature_part
    tail_weight = (
        jnp.exp(cum_log[:, -1:] - cum_log) * (reset_count == reset_count[-1])[None, :] * input_gain
    )
    block_decay = jnp.exp(cum_log[:, -1]) * (reset_count[-1] == 0)
    fresh_state = jnp.einsum(
        "sn,shp->hnp",
        write_part,
        feature_part * tail_weight.T[:, :, None],
        precision=lax.Precision.HIGHEST,
    )
    return (block_decay[:, None, None] * carry_state + fresh_state, result)


def link_states(earlier, later):
    return (earlier[0] * later[0], later[0][:, None, None] * earlier[1] + later[1])


def shards(mixer_input, write_rows, read_rows, log_decay, skip_gain, reset_offsets, grad_out):
    write_whole, read_whole = (
        lax.all_gather(write_rows, "head", axis=0, tiled=True),
        lax.all_gather(read_rows, "head", axis=0, tiled=True),
    )
    token_count = mixer_input.shape[0]
    head_count = log_decay.shape[0]
    head_width = mixer_input.shape[1] // head_count
    feature_full = mixer_input.astype(jnp.float32).reshape(token_count, head_count, head_width)
    write_full = write_whole.astype(jnp.float32)
    read_full = read_whole.astype(jnp.float32)
    cotangent = grad_out.astype(jnp.float32).reshape(token_count, head_count, head_width)
    positions = jnp.arange(token_count, dtype=jnp.int32)
    resets = jnp.any(positions[:, None] == reset_offsets[0][None, :], axis=1).astype(jnp.float32)
    cum_log = jnp.cumsum(log_decay, axis=1)
    reset_count = jnp.cumsum(resets)
    input_gain = jnp.sqrt(-jnp.expm1(2.0 * log_decay))
    tail_weight = (
        jnp.exp(cum_log[:, -1:] - cum_log) * (reset_count == reset_count[-1])[None, :] * input_gain
    )
    local_state = jnp.einsum(
        "tn,thp->hnp",
        write_full,
        feature_full * tail_weight.T[:, :, None],
        precision=lax.Precision.HIGHEST,
    )
    block_decay = jnp.exp(cum_log[:, -1]) * (reset_count[-1] == 0)
    entry_decay = jnp.exp(cum_log) * (reset_count == 0)[None, :]
    local_grad = jnp.einsum(
        "tn,thp->hnp",
        read_full,
        cotangent * entry_decay.T[:, :, None],
        precision=lax.Precision.HIGHEST,
    )
    identity = (jnp.ones_like(block_decay), jnp.zeros_like(local_state))
    decay_before, state_in = entering(
        (block_decay, local_state), "seq", link_states, identity, False
    )
    decay_after, grad_in = entering((block_decay, local_grad), "seq", link_states, identity, True)
    spans = token_count // SPAN
    log_blocks = log_decay.reshape(head_count, spans, SPAN).transpose(1, 0, 2)
    reset_blocks = resets.reshape(spans, SPAN)

    def block_forward(feature_arg, write_arg, read_arg):
        feature_blocks = feature_arg.reshape(spans, SPAN, head_count, head_width)
        write_blocks = write_arg.reshape(spans, SPAN, write_arg.shape[1])
        read_blocks = read_arg.reshape(spans, SPAN, read_arg.shape[1])

        def advance(carry_state, inputs):
            return span_update(carry_state, inputs, skip_gain)

        end_state, outputs = lax.scan(
            advance, state_in, (feature_blocks, write_blocks, read_blocks, log_blocks, reset_blocks)
        )
        return (outputs.reshape(token_count, head_count, head_width), end_state)

    outputs, pullback = jax.vjp(block_forward, feature_full, write_full, read_full)
    grad_feature, grad_write_all, grad_read_all = pullback((cotangent, grad_in))
    grad_write, grad_read = (
        lax.psum_scatter(grad_write_all, "head", scatter_dimension=0, tiled=True),
        lax.psum_scatter(grad_read_all, "head", scatter_dimension=0, tiled=True),
    )
    grad_input = grad_feature.reshape(token_count, head_count * head_width).astype(jnp.bfloat16)
    return (grad_input, grad_write, grad_read)


def solution(mesh):
    in_specs = (
        P("seq", "head"),
        P(("seq", "head"), None),
        P(("seq", "head"), None),
        P("head", "seq"),
        P("head"),
        P("seq", None),
        P("seq", "head"),
    )
    out_specs = (P("seq", "head"), P(("seq", "head"), None), P(("seq", "head"), None))
    return jax.shard_map(shards, mesh=mesh, in_specs=in_specs, out_specs=out_specs, check_vma=False)
```

profile of v0, /device:TPU:4, one launch (start us, length us, event | category | flops | bytes accessed | tf_op | source)
XLA Modules:
  0.0 574.7 jit_solution(11024643300926106177)
XLA Ops:
  14.8 3.0 copy.74
  18.5 13.6 %all_gather.28 = bf16[2048,128]{1,0:T(8,128)(2,1)S(1)} all-gather(bf16[256,128]{1,0:T(8,128)(2,1)S(1)} %copy-done.5), channel_id=1, replica_groups=mesh['seq'=32,'head'=8] {'head'}, dimensions={0}, use_global_device_ids=true | all-gather | bytes 589824 | tf_op jit(solution)/shard_map/all_gather | solution.py:62
  33.1 3.3 fusion.90
  36.5 3.0 copy.72
  40.3 13.2 %all_gather.25 = bf16[2048,128]{1,0:T(8,128)(2,1)S(1)} all-gather(bf16[256,128]{1,0:T(8,128)(2,1)S(1)} %copy-done.6), channel_id=1, replica_groups=mesh['seq'=32,'head'=8] {'head'}, dimensions={0}, use_global_device_ids=true | all-gather | bytes 589824 | tf_op jit(solution)/shard_map/all_gather | solution.py:63
  53.5 3.3 fusion.87
  60.3 74.4 %all-reduce = f32[320]{0:T(512)S(1)} all-reduce(f32[320]{0:T(512)S(1)} %dynamic-update-slice), channel_id=2, replica_groups=mesh['seq'=32,'head'=8] {'seq'}, use_global_device_ids=true, to_apply=%add | all-reduce | flops 320 | bytes 2560
  134.8 5.0 copy.94
  139.8 3.9 copy.78
  144.9 7.4 %copy.95 = f32[80,8,8,256]{3,2,1,0:T(8,128)} copy(f32[80,8,8,256]{3,1,2,0:T(8,128)} %bitcast.375) | data formatting | bytes 10485760
  155.5 115.7 %while.83 = (s32[]{:T(128)}, f32[10,128,64]{1,2,0:T(8,128)S(1)}, f32[8,128,256]{1,2,0:T(8,128)}, f32[8,10,256,256]{3,2,1,0:T(8,128)}, f32[8,10,1,256]{3,1,2,0:T(...) while((s32[]{:T(128)}, f32[10,128,64]{1,2,0:T(8,128)S(1)}, ...), condition=%wide.region_14.15_spmd.clone.clone, body=%wide.region_9.14_spmd.clone.sunk.clone | while | flops 356031040 | bytes 10219655 | solution.py:111
  158.5 3.1 multiply_dynamic-update-slice_fusion.3
  172.9 3.1 multiply_dynamic-update-slice_fusion.3
  187.5 3.0 multiply_dynamic-update-slice_fusion.3
  201.9 3.0 multiply_dynamic-update-slice_fusion.3
  216.4 3.0 multiply_dynamic-update-slice_fusion.3
  230.9 3.0 multiply_dynamic-update-slice_fusion.3
  245.3 3.0 multiply_dynamic-update-slice_fusion.3
  259.8 2.9 multiply_dynamic-update-slice_fusion.3
  271.2 42.5 %while.80 = (s32[]{:T(128)}, f32[10,128,64]{2,1,0:T(8,128)S(1)}, s32[]{:T(128)}, f32[32,10]{1,0:T(8,128)S(1)}, f32[32,10,128,64]{2,3,1,0:T(8,128)}) while((s32[]{:T(128)}, f32[10,128,64]{2,1,0:T(8,128)S(1)}, s32[]{:T(128)}, f32[32,10]{1,0:T(8,128)S(1)}, f32[32,10,128,64]{2,3,1,0:T(8,128)}) %tuple.184), condition=%wide.region_6.7_spmd.clone, body=%wide.region_5.6_spmd.sunk.clone | while | flops 163846 | bytes 2293995 | solution.py:22
  315.1 182.8 %while.82 = (s32[]{:T(128)}, f32[10,128,64]{1,2,0:T(8,128)S(1)}, bf16[8,256,10,64]{1,3,2,0:T(8,128)(2,1)}, f32[8,256,128]{2,1,0:T(8,128)S(1)}, f32[8,256,128]{2,...) while((s32[]{:T(128)}, f32[10,128,64]{1,2,0:T(8,128)S(1)}, ...), condition=%wide.region_17.18_spmd.clone, body=%wide.region_15.17_spmd.sunk.clone | while | flops 2217705472 | bytes 16956240 | solution.py:111
  315.1 3.0 constant_dynamic-slice_fusion.18
  319.6 4.2 fusion.184
  323.8 4.4 fusion.185
  337.9 3.0 constant_dynamic-slice_fusion.18
  342.4 4.2 fusion.184
  346.7 4.4 fusion.185
  360.8 3.0 constant_dynamic-slice_fusion.18
  365.3 4.2 fusion.184
  369.5 4.4 fusion.185
  383.6 3.0 constant_dynamic-slice_fusion.18
  388.1 4.2 fusion.184
  392.3 4.4 fusion.185
  406.5 3.0 constant_dynamic-slice_fusion.18
  411.0 4.2 fusion.184
  415.2 4.4 fusion.185
  429.3 3.0 constant_dynamic-slice_fusion.18
  433.8 4.2 fusion.184
  438.0 4.4 fusion.185
  452.2 3.0 constant_dynamic-slice_fusion.18
  456.7 4.2 fusion.184
  460.9 4.4 fusion.185
  475.0 3.0 constant_dynamic-slice_fusion.18
  479.5 4.2 fusion.184
  483.8 4.4 fusion.185
  499.5 3.4 copy.83
  506.3 25.5 %reduce-scatter.3.cloned.1.call-done = f32[256,128]{1,0:T(8,128)} async-done(((f32[2048,128]{1,0:T(8,128)}), f32[256,128]{1,0:T(8,128)}) %reduce-scatter.3.cloned.1.call-update) | async-done | bytes 131088 | tf_op jit(solution)/shard_map/reduce_scatter | solution.py:119
  531.9 36.3 %reduce-scatter.5.cloned.1.call-done = f32[256,128]{1,0:T(8,128)} async-done(((f32[2048,128]{1,0:T(8,128)}), f32[256,128]{1,0:T(8,128)}) %reduce-scatter.5.cloned.1.call-update) | async-done | bytes 131088 | tf_op jit(solution)/shard_map/reduce_scatter | solution.py:120
  (521 shorter events, 241.1 us)
Async XLA Ops:
  7.2 145.1 %all-gather.8.cloned.1.call-start = ((), (), s32[]{:S(2)}) async-start(), calls=%async_computation.5 | async-start | bytes 10813440 | tf_op jit(solution)/shard_map/all_gather | solution.py:13
  14.8 3.7 copy-start.5
  17.8 14.5 %copy-start.3 = (f32[10,2048]{1,0:T(8,128)S(1)}, f32[10,2048]{1,0:T(8,128)}, u32[]{:S(2)}) copy-start(f32[10,2048]{1,0:T(8,128)} %param.18) | copy-start | bytes 245764
  18.5 14.6 %copy-start = (f32[2048,640]{0,1:T(8,128)}, f32[2048,640]{0,1:T(8,128)S(1)}, u32[]{:S(2)}) copy-start(f32[2048,640]{0,1:T(8,128)S(1)} %convert_element_type.76) | copy-start | bytes 15728644
  36.5 3.8 copy-start.6
  36.5 234.6 %all-gather.6.cloned.1.call-start = ((), (), s32[]{:S(2)}) async-start(), calls=%async_computation.4 | async-start | bytes 10813440 | tf_op jit(solution)/shard_map/all_gather | solution.py:13
  39.5 14.0 %copy-start.4 = (f32[2048,10]{0,1:T(8,128)S(1)}, f32[2048,10]{0,1:T(8,128)}, u32[]{:S(2)}) copy-start(f32[2048,10]{0,1:T(8,128)} %get-tuple-element.1043) | copy-start | bytes 245764
  40.2 13.3 %copy-start.1 = (f32[2048,640]{0,1:T(8,128)}, f32[2048,640]{0,1:T(8,128)S(1)}, u32[]{:S(2)}) copy-start(f32[2048,640]{0,1:T(8,128)S(1)} %convert_element_type.74) | copy-start | bytes 15728644
  40.2 18.5 %copy-start.8 = (u32[256]{0:T(256)S(1)}, u32[256]{0:T(256)}, u32[]{:S(2)}) copy-start(u32[256]{0:T(256)} %constant.201) | copy-start | bytes 3076
  56.8 475.0 %reduce-scatter.3.cloned.1.call-start = ((), (), s32[]{:S(2)}) async-start(), calls=%async_computation.2 | async-start | bytes 1179648 | tf_op jit(solution)/shard_map/reduce_scatter | solution.py:119
  271.2 43.9 %copy-start.7 = (f32[10]{0:T(128)S(1)}, f32[10]{0:T(128)}, u32[]{:S(2)}) copy-start(f32[10]{0:T(128)} %param.19) | copy-start | bytes 124
  497.9 1.0 copy-start.2
  498.9 69.3 %reduce-scatter.5.cloned.1.call-start = ((), (), s32[]{:S(2)}) async-start(), calls=%async_computation.3 | async-start | bytes 1179648 | tf_op jit(solution)/shard_map/reduce_scatter | solution.py:120
Sparse Core Ops, SparseCore 0:
  36.6 110.4 all-gather.7
  149.7 105.9 all-gather.5
  499.0 32.8 reduce-scatter.2
  534.8 33.3 reduce-scatter.4
where the time goes:
time: 579 us; the launch traced here: 575 us
  matrix products  184 us (32%)
  local copies, waits for them, and re-layouts  124 us (21%)
  blocking collectives  101 us (17%)
  other arithmetic  78.9 us (14%)
  waiting for transfers between devices  62.2 us (11%)
  between operations  15.4 us (3%)
  loops' own time  8.71 us (2%)
    unnamed x1, blocking collectives  74.4 us
    dot_general x16, matrix products, span_update(): jnp.einsum('hts,shp->thp', weights, feature_part, precision=lax.Precision...  68.6 us
    dynamic_update_slice x32, other arithmetic, block_forward(): lax.scan(advance, state_in, (feature_blocks, write_blocks, read_blocks, l...  45.9 us
    dot_general x24, matrix products, span_update(): jnp.einsum('sn,shp->hnp', write_part, feature_part * tail_weight.T[:, :,...  39.4 us
    dynamic_slice x62, local copies, waits for them, and re-layouts, one(): lax.dynamic_index_in_dim(a, source, 0, False)  38.2 us
    dot_general x24, matrix products, span_update(): scores = jnp.dot(read_part, write_part.T, precision=lax.Precision.HIGHEST)  37.9 us
    reduce_scatter x1, waiting for transfers between devices, shards(): lax.psum_scatter(grad_read_all, 'head', scatter_dimension=0, tiled=True)  36.3 us
    dot_general x16, matrix products, span_update(): jnp.einsum('tn,hnp->thp', read_part, carry_state, precision=lax.Precision...  31.6 us
  transfers between devices with their start and end apart: 4, of which 2 were waited for; matrix products, arithmetic and copies ran while one was open for 25% of the time, Pallas kernels for 0%

commit v1 on v0

--- a/solution.py
+++ b/solution.py
@@ -1,9 +1,20 @@
+import functools
 import jax
 import jax.numpy as jnp
 from jax import lax
 from jax.sharding import PartitionSpec as P
 
 SPAN = 256
+
+
+def press_spot_up(xs, along_dim):
+    return jnp.concatenate(
+        lax.all_to_all(jnp.stack([xs for _ in range(lax.psum(1, "head"))], axis=0), "head", 0, 0),
+        axis=along_dim,
+    )
+
+
+view_the_marks = functools.partial(press_spot_up, along_dim=0)
 
 
 def entering(part, axis, combine, identity, reverse):
@@ -59,7 +70,7 @@
 
 def shards(mixer_input, write_rows, read_rows, log_decay, skip_gain, reset_offsets, grad_out):
     write_whole, read_whole = (
-        lax.all_gather(write_rows, "head", axis=0, tiled=True),
+        view_the_marks(write_rows),
         lax.all_gather(read_rows, "head", axis=0, tiled=True),
     )
     token_count = mixer_input.shape[0]

time: 579 us -> 690 us (1.19)
  waiting for transfers between devices: 62.2 us -> 163 us
  blocking collectives: 101 us -> 88.2 us
  local copies, waits for them, and re-layouts: 124 us -> 134 us
    all_gather x2, waiting for transfers between devices: 0.01 us -> 56.1 us  [entering(): gathered = jax.tree.map(lambda a: lax.all_gather(a, axis), part)]
    reduce_scatter x1, waiting for transfers between devices: 25.5 us -> 65.7 us  [shards(): lax.psum_scatter(grad_write_all, 'head', scatter_dimension=0, tiled=True)]
    all_gather x1 -> x0, blocking collectives: 13.6 us -> none  [shards(): lax.all_gather(write_rows, 'head', axis=0, tiled=True)]
    unnamed x33 -> x31, local copies, waits for them, and re-layouts: 28.9 us -> 30.1 us
  transfers between devices with their start and end apart: 4 -> 5, of which waited for: 2 -> 4; matrix products, arithmetic and copies ran while one was open for 25% -> 12% of each run, Pallas kernels for 0% -> 0%
where the time goes in v1:
time: 690 us; the launch traced here: 685 us
  matrix products  186 us (27%)
  waiting for transfers between devices  163 us (24%)
  local copies, waits for them, and re-layouts  134 us (19%)
  blocking collectives  88.2 us (13%)
  other arithmetic  85.3 us (12%)
  between operations  15.4 us (2%)
  loops' own time  8.52 us (1%)
    unnamed x1, blocking collectives  74.3 us
    dot_general x16, matrix products, span_update(): jnp.einsum('hts,shp->thp', weights, feature_part, precision=lax.Precision...  68.5 us
    reduce_scatter x1, waiting for transfers between devices, shards(): lax.psum_scatter(grad_write_all, 'head', scatter_dimension=0, tiled=True)  65.7 us
    all_gather x2, waiting for transfers between devices, entering(): gathered = jax.tree.map(lambda a: lax.all_gather(a, axis), part)  56.1 us
    dynamic_update_slice x32, other arithmetic, block_forward(): lax.scan(advance, state_in, (feature_blocks, write_blocks, read_blocks, l...  45.8 us
    dot_general x24, matrix products, span_update(): jnp.einsum('sn,shp->hnp', write_part, feature_part * tail_weight.T[:, :,...  39.3 us
    dynamic_slice x62, local copies, waits for them, and re-layouts, one(): lax.dynamic_index_in_dim(a, source, 0, False)  38.3 us
    dot_general x24, matrix products, span_update(): scores = jnp.dot(read_part, write_part.T, precision=lax.Precision.HIGHEST)  37.8 us
  transfers between devices with their start and end apart: 5, of which 4 were waited for; matrix products, arithmetic and copies ran while one was open for 12% of the time, Pallas kernels for 0%

profile of v1, /device:TPU:4, one launch (start us, length us, event | category | flops | bytes accessed | tf_op | source)
XLA Modules:
  0.0 685.1 jit_solution(9586723761965164528)
XLA Ops:
  15.4 13.8 %all_gather.22 = bf16[2048,128]{1,0:T(8,128)(2,1)S(1)} all-gather(bf16[256,128]{1,0:T(8,128)(2,1)} %param.17), channel_id=1, replica_groups=mesh['seq'=32,'head'=8] {'head'}, dimensions={0}, use_global_device_ids=true | all-gather | bytes 589824 | tf_op jit(solution)/shard_map/all_gather | solution.py:74
  35.3 3.3 fusion.84
  39.5 4.1 all-to-all-start
  43.7 3.0 copy.75
  46.7 3.0 bitcast_multiply_fusion.2
  49.7 4.3 all-to-all-done
  54.0 5.8 convolution_bitcast_fusion.4
  64.4 74.3 %all-reduce = f32[320]{0:T(512)S(1)} all-reduce(f32[320]{0:T(512)S(1)} %dynamic-update-slice), channel_id=2, replica_groups=mesh['seq'=32,'head'=8] {'seq'}, use_global_device_ids=true, to_apply=%add | all-reduce | flops 320 | bytes 2560
  138.8 5.0 copy.95
  143.8 3.9 copy.79
  148.8 7.4 %copy.96 = f32[80,8,8,256]{3,2,1,0:T(8,128)} copy(f32[80,8,8,256]{3,1,2,0:T(8,128)} %bitcast.375) | data formatting | bytes 10485760
  159.2 42.3 %while.80 = (s32[]{:T(128)}, f32[10,128,64]{2,1,0:T(8,128)S(1)}, s32[]{:T(128)}, f32[32,10]{1,0:T(8,128)S(1)}, f32[32,10,128,64]{2,3,1,0:T(8,128)}) while((s32[]{:T(128)}, f32[10,128,64]{2,1,0:T(8,128)S(1)}, s32[]{:T(128)}, f32[32,10]{1,0:T(8,128)S(1)}, f32[32,10,128,64]{2,3,1,0:T(8,128)}) %tuple.183), condition=%wide.region_6.7_spmd.clone, body=%wide.region_5.6_spmd.sunk.clone | while | flops 163846 | bytes 2293995 | solution.py:33
  201.7 56.0 %all-gather.8.cloned.1.call-done = f32[320,128,64]{1,2,0:T(8,128)} async-done(((f32[10,128,64]{1,2,0:T(8,128)}), f32[320,128,64]{1,2,0:T(8,128)}) %all-gather.8.cloned.1.call-update) | async-done | bytes 10485776 | tf_op jit(solution)/shard_map/all_gather | solution.py:24
  261.0 118.4 %while.83 = (s32[]{:T(128)}, f32[10,128,64]{1,2,0:T(8,128)S(1)}, f32[8,128,256]{1,2,0:T(8,128)}, f32[8,10,256,256]{3,2,1,0:T(8,128)}, f32[8,10,1,256]{3,1,2,0:T(...) while((s32[]{:T(128)}, f32[10,128,64]{1,2,0:T(8,128)S(1)}, ...), condition=%wide.region_14.15_spmd.clone.clone, body=%wide.region_9.14_spmd.clone.sunk.clone | while | flops 356031040 | bytes 10226307 | solution.py:122
  264.2 3.0 multiply_dynamic-update-slice_fusion.3
  279.0 3.1 multiply_dynamic-update-slice_fusion.3
  293.8 3.0 multiply_dynamic-update-slice_fusion.3
  308.5 3.0 multiply_dynamic-update-slice_fusion.3
  338.1 3.0 multiply_dynamic-update-slice_fusion.3
  352.9 3.0 multiply_dynamic-update-slice_fusion.3
  380.5 187.7 %while.82 = (s32[]{:T(128)}, f32[10,128,64]{1,2,0:T(8,128)S(1)}, bf16[8,256,10,64]{1,3,2,0:T(8,128)(2,1)}, f32[8,256,128]{2,1,0:T(8,128)S(1)}, f32[8,256,128]{2,...) while((s32[]{:T(128)}, f32[10,128,64]{1,2,0:T(8,128)S(1)}, ...), condition=%wide.region_17.18_spmd.clone, body=%wide.region_15.17_spmd.sunk.clone | while | flops 2217705472 | bytes 16956240 | solution.py:122
  380.5 3.0 constant_dynamic-slice_fusion.18
  385.0 4.2 fusion.179
  389.2 4.4 fusion.180
  403.9 3.0 constant_dynamic-slice_fusion.18
  408.4 4.2 fusion.179
  412.6 4.4 fusion.180
  427.4 3.0 constant_dynamic-slice_fusion.18
  431.9 4.2 fusion.179
  436.1 4.4 fusion.180
  450.9 3.0 constant_dynamic-slice_fusion.18
  455.4 4.2 fusion.179
  459.6 4.4 fusion.180
  474.3 3.0 constant_dynamic-slice_fusion.18
  478.8 4.2 fusion.179
  483.0 4.4 fusion.180
  497.7 3.0 constant_dynamic-slice_fusion.18
  502.2 4.2 fusion.179
  506.4 4.4 fusion.180
  521.1 3.0 constant_dynamic-slice_fusion.18
  525.6 4.2 fusion.179
  529.8 4.4 fusion.180
  544.5 3.0 constant_dynamic-slice_fusion.18
  549.0 4.2 fusion.179
  553.2 4.4 fusion.180
  569.8 3.4 copy.84
  576.7 65.7 %reduce-scatter.3.cloned.1.call-done = f32[256,128]{1,0:T(8,128)} async-done(((f32[2048,128]{1,0:T(8,128)}), f32[256,128]{1,0:T(8,128)}) %reduce-scatter.3.cloned.1.call-update) | async-done | bytes 131088 | tf_op jit(solution)/shard_map/reduce_scatter | solution.py:130
  642.4 36.2 %reduce-scatter.5.cloned.1.call-done = f32[256,128]{1,0:T(8,128)} async-done(((f32[2048,128]{1,0:T(8,128)}), f32[256,128]{1,0:T(8,128)}) %reduce-scatter.5.cloned.1.call-update) | async-done | bytes 131088 | tf_op jit(solution)/shard_map/reduce_scatter | solution.py:131
  (522 shorter events, 263.8 us)
Async XLA Ops:
  7.2 152.0 %all-gather.6.cloned.1.call-start = ((), (), s32[]{:S(2)}) async-start(), calls=%async_computation.5 | async-start | bytes 10813440 | tf_op jit(solution)/shard_map/all_gather | solution.py:24
  32.2 1.6 copy-start.2
  32.9 2.4 copy-start
  32.9 5.7 copy-start.3
  39.5 14.5 %all-to-all-start = ((bf16[8,256,128]{2,1,0:T(8,128)(2,1)}), bf16[8,256,128]{2,1,0:T(8,128)(2,1)}, u32[]{:S(2)}, u32[]{:S(2)}) async-start(bf16[8,256,128]{2,1,0:T(8,128)(2,1)} %stack.2), calls=%async_computation | async-start | bytes 1048576 | tf_op jit(solution)/shard_map/all_to_all | solution.py:12
  43.6 214.2 %all-gather.8.cloned.1.call-start = ((), (), s32[]{:S(2)}) async-start(), calls=%async_computation.6 | async-start | bytes 10813440 | tf_op jit(solution)/shard_map/all_gather | solution.py:24
  59.8 3.1 copy-start.7
  59.8 4.3 copy-start.6
  59.8 582.6 %reduce-scatter.3.cloned.1.call-start = ((), (), s32[]{:S(2)}) async-start(), calls=%async_computation.3 | async-start | bytes 1179648 | tf_op jit(solution)/shard_map/reduce_scatter | solution.py:130
  143.8 4.9 copy-start.4
  261.0 119.5 %copy-start.5 = (f32[10]{0:T(128)S(1)}, f32[10]{0:T(128)}, u32[]{:S(2)}) copy-start(f32[10]{0:T(128)} %param.19) | copy-start | bytes 124
  568.2 1.0 copy-start.1
  569.3 109.4 %reduce-scatter.5.cloned.1.call-start = ((), (), s32[]{:S(2)}) async-start(), calls=%async_computation.4 | async-start | bytes 1179648 | tf_op jit(solution)/shard_map/reduce_scatter | solution.py:131
Sparse Core Ops, SparseCore 0:
  38.7 110.5 all-gather.5
  151.8 105.8 all-gather.7
  569.4 72.9 reduce-scatter.2
  645.3 33.2 reduce-scatter.4
